TPU v7x, 32 devices: a whole 2x2x4 slice. The times are simulated.
32 devices in a mesh: win: 2 (over y), row: 4 (over z), col: 4 (over x, core).
Axes of the slice: x: 2, y: 2, z: 4, core: 2. Of those that a mesh axis runs over, the one named last changes fastest.
Arguments:
- records: bfloat16 [32, 4096, 1024], P('win', ('row', 'col'))
- tile_pairs: int32 [4, 4, 4, 2], P('row', 'col'), may hold values from 0 to 3
- tile_count: int32 [4, 4], P('row', 'col'), may hold values from 1 to 4, as said below
- bin_index: int32 [32], replicated, may hold values from 1 to 511, as said below
Outputs:
- cross_tiles: bfloat16 [4, 4, 4, 2, 32, 256, 256], P('row', 'col', 'win')
Inputs may be any that keep to these rules, and one draw needn't show every extreme that they name: Slots 0 to tile_count - 1 of a cell are live; some cell has all 4 live and some cell one. `bin_index`: distinct and increasing; the first is 1 and the last 511.
All inputs are finite; a program needn't handle non-finite values.
Results may differ from a plain program's by a relative error of at most 0.0069.
Values may be sent and summed in bfloat16 or wider, within the bound.
A program may use at most 256 MiB of HBM per device.

v0:
```python
import math
import jax
import jax.numpy as jnp
from jax import lax
from jax.sharding import PartitionSpec as P


def dft_table(bin_index, length):
    sample_ids = jnp.arange(length, dtype=jnp.int32)
    phases = sample_ids[:, None] * bin_index[None, :] % length
    angles = 2.0 * math.pi / length * phases.astype(jnp.float32)
    window_taper = 0.5 - 0.5 * jnp.cos(2.0 * math.pi / length * sample_ids.astype(jnp.float32))
    cosine = window_taper[:, None] * jnp.cos(angles)
    sine = -window_taper[:, None] * jnp.sin(angles)
    return jnp.concatenate([cosine, sine], axis=1).astype(jnp.bfloat16)


def cross_spectra(first_block, second_block):
    second_real = second_block[:, 0]
    second_imag = second_block[:, 1]
    stacked = jnp.stack(
        [
            jnp.stack([second_real, second_imag], axis=1),
            jnp.stack([-second_imag, second_real], axis=1),
        ],
        axis=0,
    )
    return jnp.einsum(
        "wcktp,ewcktq->tekpq", first_block, stacked, preferred_element_type=jnp.float32
    )


def body(records, tile_pairs, tile_count, bin_index):
    length = records.shape[2]
    chan_block = records.shape[1]
    kept_bins = bin_index.shape[0]
    phase_table = dft_table(bin_index, length)
    spectrum = jnp.einsum("wcs,sk->wkc", records, phase_table, preferred_element_type=jnp.float32)
    energy = jnp.sqrt(jnp.mean(spectrum * spectrum, axis=1, keepdims=True) + 1e-06)
    whitened = (spectrum / energy).astype(jnp.bfloat16)
    whitened = lax.all_gather(whitened, "win", axis=0, tiled=True)
    row_set = lax.all_gather(whitened, "col", axis=2, tiled=True)
    column_set = lax.all_gather(whitened, "row", axis=2, tiled=True)
    window_rows = whitened.shape[0]
    row_blocks = row_set.reshape(window_rows, 2, kept_bins, lax.axis_size("col"), chan_block)
    column_blocks = column_set.reshape(window_rows, 2, kept_bins, lax.axis_size("row"), chan_block)
    slot_pairs = tile_pairs[0, 0]
    live_count = tile_count[0, 0]
    owned_slots = slot_pairs.shape[0] // lax.axis_size("win")
    begin_row = lax.axis_index("win") * owned_slots
    chosen = lax.dynamic_slice_in_dim(slot_pairs, begin_row, owned_slots, 0)
    positions = begin_row + jnp.arange(owned_slots, dtype=jnp.int32)
    first_chosen = jnp.take(row_blocks, chosen[:, 0], axis=3)
    second_chosen = jnp.take(column_blocks, chosen[:, 1], axis=3)
    live_mask = (positions < live_count).astype(jnp.float32)
    summed = cross_spectra(first_chosen, second_chosen) * live_mask[:, None, None, None, None]
    return summed.astype(jnp.bfloat16).reshape(
        1, 1, owned_slots, 2, kept_bins, chan_block, chan_block
    )


def solution(mesh):
    return jax.shard_map(
        body,
        mesh=mesh,
        in_specs=(
            P("win", ("row", "col"), None),
            P("row", "col", None, None),
            P("row", "col"),
            P(),
        ),
        out_specs=P("row", "col", "win", None, None, None, None),
        check_vma=False,
    )
```

profile of v0, /device:TPU:0, one launch (start us, length us, event | category | flops | bytes accessed | tf_op | source)
XLA Modules:
  0.0 217.1 jit_solution(18415207110802437952)
XLA Ops:
  6.5 0.0 copy-start
  6.5 0.0 all-gather.4.cloned.1.call-start
  6.6 1.3 multiply_convert_fusion.1
  7.8 6.1 %multiply_reduce_fusion = (f32[16,256]{1,0:T(8,128)S(1)}, f32[64,16,256]{2,0,1:T(8,128)S(1)}) fusion(bf16[16,256,1024]{2,1,0:T(8,128)(2,1)} %param.6, bf16[1024,32]{0,1:T(8,128)(2,1)S(1)} %get-tuple-element.13, bf16[1024,32]{0,1:T(8,128)(2,1)S(1)} %get-tuple-element.12), kind=kOutput, calls=%fused_computation.14 | convolution fusion | flops 537653248 | bytes 9584640 | tf_op jit(solution)/shard_map/wcs,sk->wkc/dot_general | solution.py:38
  13.9 0.9 fusion.8
  14.8 0.0 all-gather.4.cloned.1.call-update
  14.9 0.0 all-gather.6.cloned.1.call-start
  14.9 24.1 %all-gather.4.cloned.1.call-done = bf16[32,64,256]{2,1,0:T(8,128)(2,1)} async-done(((bf16[16,64,256]{2,1,0:T(8,128)(2,1)}), bf16[32,64,256]{2,1,0:T(8,128)(2,1)}) %all-gather.4.cloned.1.call-update) | async-done | bytes 1048592 | tf_op jit(solution)/shard_map/all_gather | solution.py:41
  39.0 0.0 all-gather.6.cloned.1.call-update
  39.0 0.0 all-gather.8.cloned.1.call-start
  39.1 0.7 all-gather.8.cloned.1.call-update
  40.4 0.0 copy-done
  40.4 0.1 constant_dynamic-slice_fusion
  40.5 0.1 copy.20
  40.6 0.2 slice_reduce_fusion
  40.9 80.3 %all-gather.6.cloned.1.call-done = bf16[32,64,1024]{2,1,0:T(8,128)(2,1)} async-done(((bf16[32,64,256]{2,1,0:T(8,128)(2,1)}), bf16[32,64,1024]{2,1,0:T(8,128)(2,1)}) %all-gather.6.cloned.1.call-update) | async-done | bytes 4194320 | tf_op jit(solution)/shard_map/all_gather | solution.py:43
  121.2 7.9 %reshape.42 = bf16[32,2,32,4,256]{4,3,2,1,0:T(4,128)(2,1)} reshape(bf16[32,64,1024]{2,1,0:T(8,128)(2,1)} %all-gather.6.cloned.1.call-done) | data formatting | bytes 8388608 | tf_op jit(solution)/shard_map/reshape | solution.py:46
  129.1 5.3 %copy.21 = bf16[32,2,32,4,256]{4,2,1,0,3:T(8,128)(2,1)} copy(bf16[32,2,32,4,256]{4,3,2,1,0:T(4,128)(2,1)} %reshape.42) | data formatting | bytes 8388608 | tf_op jit(solution)/shard_map/reshape | solution.py:46
  134.4 21.6 %all-gather.8.cloned.1.call-done = bf16[32,64,1024]{2,1,0:T(8,128)(2,1)} async-done(((bf16[32,64,256]{2,1,0:T(8,128)(2,1)}), bf16[32,64,1024]{2,1,0:T(8,128)(2,1)}) %all-gather.8.cloned.1.call-update) | async-done | bytes 4194320 | tf_op jit(solution)/shard_map/all_gather | solution.py:42
  156.0 7.8 %reshape.43 = bf16[32,2,32,4,256]{4,3,2,1,0:T(4,128)(2,1)} reshape(bf16[32,64,1024]{2,1,0:T(8,128)(2,1)} %all-gather.8.cloned.1.call-done) | data formatting | bytes 8388608 | tf_op jit(solution)/shard_map/reshape | solution.py:45
  163.8 4.9 %copy.24 = bf16[32,2,32,4,256]{4,2,1,0,3:T(8,128)(2,1)} copy(bf16[32,2,32,4,256]{4,3,2,1,0:T(4,128)(2,1)} %reshape.43) | data formatting | bytes 8388608 | tf_op jit(solution)/shard_map/reshape | solution.py:45
  168.8 2.9 %gather_fusion = bf16[2,32,2,32,256]{4,3,2,1,0:T(8,128)(2,1)S(1)} fusion(bf16[32,2,32,4,256]{4,2,1,0,3:T(8,128)(2,1)} %copy.21, s32[1024]{0:T(1024)S(1)} %pad_clamp_fusion.1), kind=kCustom, calls=%fused_computation.clone | custom fusion | bytes 4194312 | tf_op jit(solution)/shard_map/jit(_take)/gather | solution.py:54
  171.6 2.7 %fusion.6 = (bf16[1,32,2,32,2,256]{5,1,2,0,3,4:T(8,128)(2,1)}, bf16[32,2,32,2,256]{4,0,1,2,3:T(8,128)(2,1)S(1)}) fusion(bf16[2,32,2,32,256]{4,3,2,1,0:T(8,128)(2,1)S(1)} %gather_fusion, pred[2]{0:T(512)(128)(4,1)S(1)} %get-tuple-element.19), kind=kLoop, calls=%fused_computation.15 | loop fusion | flops 1048576 | bytes 6291458 | tf_op jit(solution)/shard_map/stack | solution.py:21
  174.3 1.1 slice_negate_fusion
  175.4 2.9 %gather_fusion.1 = bf16[2,32,2,32,256]{4,3,2,1,0:T(8,128)(2,1)S(1)} fusion(bf16[32,2,32,4,256]{4,2,1,0,3:T(8,128)(2,1)} %copy.24, s32[1024]{0:T(1024)S(1)} %pad_clamp_fusion), kind=kCustom, calls=%fused_computation.1.clone | custom fusion | bytes 4194312 | tf_op jit(solution)/shard_map/jit(_take)/gather | solution.py:53
  178.3 0.0 copy-start.2
  178.3 0.3 select_bitcast_fusion
  178.5 0.9 copy-done.2
  179.5 0.0 copy-start.3
  179.5 0.2 maximum_bitcast_fusion
  179.7 1.3 copy-done.3
  181.1 8.2 %fusion.1 = bf16[1,1,2,2,32,256,256]{5,6,3,4,2,1,0:T(8,128)(2,1)} fusion(f32[2]{0:T(128)S(1)} %compare_convert_fusion, bf16[1,32,2,32,2,256]{5,1,2,0,3,4:T(8,128)(2,1)S(1)} %maximum_bitcast_fusion, bf16[1,32,2,32,2,256]{5,1,2,0,3,4:T(8,128)(2,1)S(1)} %copy-done.3, bf16[32,2,32,2,256,1]{4,2,1,0,3,5:T(8,128)(2,1)S(1)} %select_bitcast_fusion), kind=kOutput, calls=%fused_computation.4 | convolution fusion | flops 1092616192 | bytes 23068680 | tf_op jit(solution)/shard_map/wcktp,ewcktq->tekpq/dot_general | solution.py:28
  189.3 0.0 copy-start.1
  189.3 21.2 %copy.26 = bf16[1,1,2,2,32,256,256]{6,5,4,3,2,1,0:T(8,128)(2,1)} copy(bf16[1,1,2,2,32,256,256]{5,6,3,4,2,1,0:T(8,128)(2,1)} %fusion.1) | data formatting | bytes 33554432 | tf_op jit(solution)/shard_map/reshape | solution.py:57
  210.5 0.0 copy-done.1
  (8 shorter events, 0.1 us)
Async XLA Ops:
  6.5 33.9 %copy-start = (s32[1,1,4,2]{2,3,1,0:T(2,128)S(1)}, s32[1,1,4,2]{2,3,1,0:T(2,128)}, u32[]{:S(2)}) copy-start(s32[1,1,4,2]{2,3,1,0:T(2,128)} %param.7) | copy-start | bytes 100
  6.5 32.5 %all-gather.4.cloned.1.call-start = ((), (), s32[]{:S(2)}) async-start(), calls=%async_computation | async-start | bytes 1572864 | tf_op jit(solution)/shard_map/all_gather | solution.py:41
  14.9 106.3 %all-gather.6.cloned.1.call-start = ((), (), s32[]{:S(2)}) async-start(), calls=%async_computation.1 | async-start | bytes 5242880 | tf_op jit(solution)/shard_map/all_gather | solution.py:43
  39.0 116.9 %all-gather.8.cloned.1.call-start = ((), (), s32[]{:S(2)}) async-start(), calls=%async_computation.2 | async-start | bytes 5242880 | tf_op jit(solution)/shard_map/all_gather | solution.py:42
  178.3 1.2 copy-start.2
  179.5 1.6 copy-start.3
  189.3 21.2 %copy-start.1 = (s32[1,1,4,2]{2,3,1,0:T(2,128)S(1)}, s32[1,1,4,2]{2,3,1,0:T(2,128)}, u32[]{:S(2)}) copy-start(s32[1,1,4,2]{2,3,1,0:T(2,128)} %param.7) | copy-start | bytes 100
Sparse Core Ops, SparseCore 0:
  15.0 23.9 all-gather.3
  40.6 80.5 all-gather.5
  122.7 33.1 all-gather.7
where the time goes:
time: 218 us; the launch traced here: 217 us
  waiting for transfers between devices  127 us (58%)
  local copies, waits for them, and re-layouts  55.6 us (26%)
  matrix products  14.3 us (7%)
  between operations  13.9 us (6%)
  other arithmetic  6.51 us (3%)
    all_gather x1, waiting for transfers between devices, body(): column_set = lax.all_gather(whitened, 'row', axis=2, tiled=True)  80.3 us
    all_gather x1, waiting for transfers between devices, body(): whitened = lax.all_gather(whitened, 'win', axis=0, tiled=True)  24.1 us
    all_gather x1, waiting for transfers between devices, body(): row_set = lax.all_gather(whitened, 'col', axis=2, tiled=True)  21.6 us
    reshape x1, local copies, waits for them, and re-layouts, body(): summed.astype(jnp.bfloat16)  21.2 us
    reshape x2, local copies, waits for them, and re-layouts, body(): column_set.reshape(window_rows, 2, kept_bins, lax.axis_size('row'), chan_...  13.2 us
    reshape x2, local copies, waits for them, and re-layouts, body(): row_set.reshape(window_rows, 2, kept_bins, lax.axis_size('col'), chan_block)  12.8 us
    dot_general x1, matrix products, cross_spectra(): jnp.einsum('wcktp,ewcktq->tekpq', first_block, stacked, preferred_element...  8.24 us
    dot_general x1, matrix products, body(): jnp.einsum('wcs,sk->wkc', records, phase_table, preferred_element_type=jn...  6.06 us
  transfers between devices with their start and end apart: 3, of which 3 were waited for; matrix products, arithmetic and copies ran while one was open for 6% of the time, Pallas kernels for 0%

commit v1 on v0

--- a/solution.py
+++ b/solution.py
@@ -40,7 +40,27 @@
     whitened = (spectrum / energy).astype(jnp.bfloat16)
     whitened = lax.all_gather(whitened, "win", axis=0, tiled=True)
     row_set = lax.all_gather(whitened, "col", axis=2, tiled=True)
-    column_set = lax.all_gather(whitened, "row", axis=2, tiled=True)
+
+    def order_kinds(block_in, row_axis):
+        n_axis = lax.axis_size(row_axis)
+        earlier = map(lambda q: (q, (q + 1) % n_axis), range(n_axis))
+        panels = list(map(lambda q: (q, (q - 1) % n_axis), range(n_axis)))
+        prior, k_now = ([block_in], [block_in])
+        found = list(earlier)
+        for _ in range(n_axis // 2):
+            arr_out = lax.ppermute(prior[-1], axis_name=row_axis, perm=found)
+            prior.append(arr_out)
+        j0 = 0
+        while j0 < (n_axis - 1) // 2:
+            k_now.append(lax.ppermute(k_now[-1], axis_name=row_axis, perm=panels))
+            j0 = j0 + 1
+        extra = jnp.concatenate([*prior[::-1], *k_now[1:]], axis=2)
+        later = jnp.roll(
+            extra, (lax.axis_index(row_axis) - n_axis // 2) * block_in.shape[2], axis=2
+        )
+        return later
+
+    column_set = order_kinds(whitened, "row")
     window_rows = whitened.shape[0]
     row_blocks = row_set.reshape(window_rows, 2, kept_bins, lax.axis_size("col"), chan_block)
     column_blocks = column_set.reshape(window_rows, 2, kept_bins, lax.axis_size("row"), chan_block)

time: 218 us -> 192 us (0.88)
  waiting for transfers between devices: 127 us -> 91.8 us
  starting transfers between devices: 0.08 us -> 5.46 us
  local copies, waits for them, and re-layouts: 55.6 us -> 58.7 us
    all_gather x1 -> x0, waiting for transfers between devices: 80.3 us -> none  [body(): column_set = lax.all_gather(whitened, 'row', axis=2, tiled=True)]
    ppermute x0 -> x3, waiting for transfers between devices: none -> 67.7 us  [the longest x2 48.4 us: order_kinds(): arr_out = lax.ppermute(prior[-1], axis_name=row_axis, perm=found)]
    all_gather x1, waiting for transfers between devices: 21.6 us -> 0.01 us  [body(): row_set = lax.all_gather(whitened, 'col', axis=2, tiled=True)]
    ppermute x0 -> x3, starting transfers between devices: none -> 5.41 us  [the longest x1 3.87 us: order_kinds(): k_now.append(lax.ppermute(k_now[-1], axis_name=row_axis, perm=panels))]
    dynamic_slice x0 -> x1, local copies, waits for them, and re-layouts: none -> 2.68 us  [order_kinds(): jnp.roll(extra, (lax.axis_index(row_axis) - n_axis // 2) * block_in.shape...]
  transfers between devices with their start and end apart: 3 -> 5, of which waited for: 3 -> 4; matrix products, arithmetic and copies ran while one was open for 6% -> 13% of each run, Pallas kernels for 0% -> 0%
where the time goes in v1:
time: 192 us; the launch traced here: 191 us
  waiting for transfers between devices  91.8 us (48%)
  local copies, waits for them, and re-layouts  58.7 us (31%)
  matrix products  14.3 us (7%)
  between operations  14.2 us (7%)
  other arithmetic  6.83 us (4%)
  starting transfers between devices  5.46 us (3%)
    ppermute x2, waiting for transfers between devices, order_kinds(): arr_out = lax.ppermute(prior[-1], axis_name=row_axis, perm=found)  48.4 us
    all_gather x1, waiting for transfers between devices, body(): whitened = lax.all_gather(whitened, 'win', axis=0, tiled=True)  24.1 us
    reshape x1, local copies, waits for them, and re-layouts, body(): summed.astype(jnp.bfloat16)  21.2 us
    ppermute x1, waiting for transfers between devices, order_kinds(): k_now.append(lax.ppermute(k_now[-1], axis_name=row_axis, perm=panels))  19.3 us
    reshape x2, local copies, waits for them, and re-layouts, body(): column_set.reshape(window_rows, 2, kept_bins, lax.axis_size('row'), chan_...  12.9 us
    reshape x2, local copies, waits for them, and re-layouts, body(): row_set.reshape(window_rows, 2, kept_bins, lax.axis_size('col'), chan_block)  12.8 us
    dot_general x1, matrix products, cross_spectra(): jnp.einsum('wcktp,ewcktq->tekpq', first_block, stacked, preferred_element...  8.24 us
    dot_general x1, matrix products, body(): jnp.einsum('wcs,sk->wkc', records, phase_table, preferred_element_type=jn...  6.06 us
  transfers between devices with their start and end apart: 5, of which 4 were waited for; matrix products, arithmetic and copies ran while one was open for 13% of the time, Pallas kernels for 0%

profile of v1, /device:TPU:0, one launch (start us, length us, event | category | flops | bytes accessed | tf_op | source)
XLA Modules:
  0.0 191.3 jit_solution(15525399527534338954)
XLA Ops:
  6.5 0.0 copy-start
  6.5 0.0 all-gather.3.cloned.1.call-start
  6.6 1.3 multiply_convert_fusion.1
  7.8 6.1 %multiply_reduce_fusion = (f32[16,256]{1,0:T(8,128)S(1)}, f32[64,16,256]{2,0,1:T(8,128)S(1)}) fusion(bf16[16,256,1024]{2,1,0:T(8,128)(2,1)} %param.6, bf16[1024,32]{0,1:T(8,128)(2,1)S(1)} %get-tuple-element.13, bf16[1024,32]{0,1:T(8,128)(2,1)S(1)} %get-tuple-element.12), kind=kOutput, calls=%fused_computation.14 | convolution fusion | flops 537653248 | bytes 9584640 | tf_op jit(solution)/shard_map/wcs,sk->wkc/dot_general | solution.py:38
  13.9 0.9 fusion.8
  14.8 0.0 all-gather.3.cloned.1.call-update
  14.9 0.0 all-gather.5.cloned.1.call-start
  14.9 24.1 %all-gather.3.cloned.1.call-done = bf16[32,64,256]{2,1,0:T(8,128)(2,1)} async-done(((bf16[16,64,256]{2,1,0:T(8,128)(2,1)}), bf16[32,64,256]{2,1,0:T(8,128)(2,1)}) %all-gather.3.cloned.1.call-update) | async-done | bytes 1048592 | tf_op jit(solution)/shard_map/all_gather | solution.py:41
  39.0 0.0 copy-start.2
  39.0 0.0 all-gather.5.cloned.1.call-update
  39.1 1.5 collective-permute-start
  40.6 0.0 copy-done
  40.6 0.1 constant_dynamic-slice_fusion
  40.7 0.1 copy.27
  40.8 25.2 %collective-permute-done = bf16[32,64,256]{2,1,0:T(8,128)(2,1)S(1)} collective-permute-done((bf16[32,64,256]{2,1,0:T(8,128)(2,1)}, bf16[32,64,256]{2,1,0:T(8,128)(2,1)S(1)}, u32[]{:S(2)}, u32[]{:S(2)}) %collective-permute-start) | collective-permute-done | bytes 1048608 | tf_op jit(solution)/shard_map/ppermute | solution.py:51
  66.0 0.0 collective-permute-start.1
  66.0 0.2 slice_reduce_fusion
  66.9 3.9 %collective-permute-start.2 = (bf16[32,64,256]{2,1,0:T(8,128)(2,1)}, bf16[32,64,256]{2,1,0:T(8,128)(2,1)S(1)}, u32[]{:S(2)}, u32[]{:S(2)}) collective-permute-start(bf16[32,64,256]{2,1,0:T(8,128)(2,1)} %all-gather.3.cloned.1.call-done), channel_id=1, source_target_pairs={{0,12},{4,0},{8,4},{12,8},{1,13},{5,1},{9,5},{13,9},{2,14},{6,2},{... | collective-permute-start | bytes 3145736 | tf_op jit(solution)/shard_map/ppermute | solution.py:55
  70.8 23.1 %collective-permute-done.1 = bf16[32,64,256]{2,1,0:T(8,128)(2,1)S(1)} collective-permute-done((bf16[32,64,256]{2,1,0:T(8,128)(2,1)S(1)}, bf16[32,64,256]{2,1,0:T(8,128)(2,1)S(1)}, u32[]{:S(2)}, u32[]{:S(2)}) %collective-permute-start.1) | collective-permute-done | bytes 1048608 | tf_op jit(solution)/shard_map/ppermute | solution.py:51
  93.9 0.1 constant_dynamic-update-slice_fusion.7
  94.1 0.1 constant_dynamic-update-slice_fusion.6
  94.2 0.0 copy-done.2
  94.2 0.1 constant_dynamic-update-slice_fusion.5
  94.4 19.3 %collective-permute-done.2 = bf16[32,64,256]{2,1,0:T(8,128)(2,1)S(1)} collective-permute-done((bf16[32,64,256]{2,1,0:T(8,128)(2,1)}, bf16[32,64,256]{2,1,0:T(8,128)(2,1)S(1)}, u32[]{:S(2)}, u32[]{:S(2)}) %collective-permute-start.2) | collective-permute-done | bytes 1048608 | tf_op jit(solution)/shard_map/ppermute | solution.py:55
  113.7 0.1 constant_dynamic-update-slice_fusion.4
  113.8 0.1 constant_dynamic-update-slice_fusion.3
  113.9 0.1 constant_dynamic-update-slice_fusion.2
  114.1 0.1 constant_dynamic-update-slice_fusion.1
  114.2 0.1 constant_dynamic-update-slice_fusion
  114.4 2.7 %constant_dynamic-slice_fusion.1 = bf16[32,64,1024]{2,1,0:T(8,128)(2,1)} fusion(bf16[32,64,2048]{2,1,0:T(8,128)(2,1)S(1)} %constant_dynamic-update-slice_fusion, s32[]{:T(128)S(6)} %select_n.31), kind=kLoop, calls=%fused_computation.54 | loop fusion | bytes 8388612 | tf_op jit(solution)/shard_map/jit(_roll_dynamic)/dynamic_slice | solution.py:58
  117.1 7.9 %reshape.42 = bf16[32,2,32,4,256]{4,3,2,1,0:T(4,128)(2,1)} reshape(bf16[32,64,1024]{2,1,0:T(8,128)(2,1)} %constant_dynamic-slice_fusion.1) | data formatting | bytes 8388608 | tf_op jit(solution)/shard_map/reshape | solution.py:66
  125.0 5.0 %copy.28 = bf16[32,2,32,4,256]{4,2,1,0,3:T(8,128)(2,1)} copy(bf16[32,2,32,4,256]{4,3,2,1,0:T(4,128)(2,1)} %reshape.42) | data formatting | bytes 8388608 | tf_op jit(solution)/shard_map/reshape | solution.py:66
  130.0 2.9 %gather_fusion = bf16[2,32,2,32,256]{4,3,2,1,0:T(8,128)(2,1)S(1)} fusion(bf16[32,2,32,4,256]{4,2,1,0,3:T(8,128)(2,1)} %copy.28, s32[1024]{0:T(1024)S(1)} %pad_clamp_fusion.1), kind=kCustom, calls=%fused_computation.clone | custom fusion | bytes 4194312 | tf_op jit(solution)/shard_map/jit(_take)/gather | solution.py:74
  132.9 2.7 %fusion.6 = (bf16[1,32,2,32,2,256]{5,1,2,0,3,4:T(8,128)(2,1)}, bf16[32,2,32,2,256]{4,0,1,2,3:T(8,128)(2,1)S(1)}) fusion(bf16[2,32,2,32,256]{4,3,2,1,0:T(8,128)(2,1)S(1)} %gather_fusion, pred[2]{0:T(512)(128)(4,1)S(1)} %get-tuple-element.19), kind=kLoop, calls=%fused_computation.15 | loop fusion | flops 1048576 | bytes 6291458 | tf_op jit(solution)/shard_map/stack | solution.py:21
  135.5 0.1 slice_negate_fusion
  135.6 1.5 maximum_bitcast_fusion
  137.2 0.0 all-gather.5.cloned.1.call-done
  137.2 7.8 %reshape.43 = bf16[32,2,32,4,256]{4,3,2,1,0:T(4,128)(2,1)} reshape(bf16[32,64,1024]{2,1,0:T(8,128)(2,1)} %all-gather.5.cloned.1.call-done) | data formatting | bytes 8388608 | tf_op jit(solution)/shard_map/reshape | solution.py:65
  145.0 4.9 %copy.31 = bf16[32,2,32,4,256]{4,2,1,0,3:T(8,128)(2,1)} copy(bf16[32,2,32,4,256]{4,3,2,1,0:T(4,128)(2,1)} %reshape.43) | data formatting | bytes 8388608 | tf_op jit(solution)/shard_map/reshape | solution.py:65
  149.9 2.9 %gather_fusion.1 = bf16[2,32,2,32,256]{4,3,2,1,0:T(8,128)(2,1)S(1)} fusion(bf16[32,2,32,4,256]{4,2,1,0,3:T(8,128)(2,1)} %copy.31, s32[1024]{0:T(1024)S(1)} %pad_clamp_fusion), kind=kCustom, calls=%fused_computation.1.clone | custom fusion | bytes 4194312 | tf_op jit(solution)/shard_map/jit(_take)/gather | solution.py:73
  152.8 0.0 copy-start.3
  152.8 0.0 copy-start.4
  152.8 0.3 select_bitcast_fusion
  153.1 1.3 copy-done.3
  154.4 0.6 copy-done.4
  155.0 8.2 %fusion.1 = bf16[1,1,2,2,32,256,256]{5,6,3,4,2,1,0:T(8,128)(2,1)} fusion(f32[2]{0:T(128)S(1)} %compare_convert_fusion, bf16[1,32,2,32,2,256]{5,1,2,0,3,4:T(8,128)(2,1)S(1)} %copy-done.4, bf16[1,32,2,32,2,256]{5,1,2,0,3,4:T(8,128)(2,1)S(1)} %copy-done.3, bf16[32,2,32,2,256,1]{4,2,1,0,3,5:T(8,128)(2,1)S(1)} %select_bitcast_fusion), kind=kOutput, calls=%fused_computation.4 | convolution fusion | flops 1092616192 | bytes 23068680 | tf_op jit(solution)/shard_map/wcktp,ewcktq->tekpq/dot_general | solution.py:28
  163.3 0.0 copy-start.1
  163.3 21.2 %copy.33 = bf16[1,1,2,2,32,256,256]{6,5,4,3,2,1,0:T(8,128)(2,1)} copy(bf16[1,1,2,2,32,256,256]{5,6,3,4,2,1,0:T(8,128)(2,1)} %fusion.1) | data formatting | bytes 33554432 | tf_op jit(solution)/shard_map/reshape | solution.py:77
  184.5 0.0 copy-done.1
  (8 shorter events, 0.1 us)
Async XLA Ops:
  6.5 34.1 %copy-start = (s32[1,1,4,2]{2,3,1,0:T(2,128)S(1)}, s32[1,1,4,2]{2,3,1,0:T(2,128)}, u32[]{:S(2)}) copy-start(s32[1,1,4,2]{2,3,1,0:T(2,128)} %param.7) | copy-start | bytes 100
  6.5 32.5 %all-gather.3.cloned.1.call-start = ((), (), s32[]{:S(2)}) async-start(), calls=%async_computation | async-start | bytes 1572864 | tf_op jit(solution)/shard_map/all_gather | solution.py:41
  14.9 122.3 %all-gather.5.cloned.1.call-start = ((), (), s32[]{:S(2)}) async-start(), calls=%async_computation.1 | async-start | bytes 5242880 | tf_op jit(solution)/shard_map/all_gather | solution.py:42
  39.0 55.2 %copy-start.2 = (bf16[32,64,256]{2,1,0:T(8,128)(2,1)S(1)}, bf16[32,64,256]{2,1,0:T(8,128)(2,1)}, u32[]{:S(2)}) copy-start(bf16[32,64,256]{2,1,0:T(8,128)(2,1)} %all-gather.3.cloned.1.call-done) | copy-start | bytes 3145732
  39.1 27.0 %collective-permute-start = (bf16[32,64,256]{2,1,0:T(8,128)(2,1)}, bf16[32,64,256]{2,1,0:T(8,128)(2,1)S(1)}, u32[]{:S(2)}, u32[]{:S(2)}) collective-permute-start(bf16[32,64,256]{2,1,0:T(8,128)(2,1)} %all-gather.3.cloned.1.call-done), channel_id=1, source_target_pairs={{0,4},{4,8},{8,12},{12,0},{1,5},{5,9},{9,13},{13,1},{2,6},{6,10},{... | collective-permute-start | bytes 3145736 | tf_op jit(solution)/shard_map/ppermute | solution.py:51
  66.0 27.9 %collective-permute-start.1 = (bf16[32,64,256]{2,1,0:T(8,128)(2,1)S(1)}, bf16[32,64,256]{2,1,0:T(8,128)(2,1)S(1)}, u32[]{:S(2)}, u32[]{:S(2)}) collective-permute-start(bf16[32,64,256]{2,1,0:T(8,128)(2,1)S(1)} %collective-permute-done), channel_id=1, source_target_pairs={{0,4},{4,8},{8,12},{12,0},{1,5},{5,9},{9,13},{13,1},{2,6},{6,10},{... | collective-permute-start | bytes 3145736 | tf_op jit(solution)/shard_map/ppermute | solution.py:51
  66.9 46.8 %collective-permute-start.2 = (bf16[32,64,256]{2,1,0:T(8,128)(2,1)}, bf16[32,64,256]{2,1,0:T(8,128)(2,1)S(1)}, u32[]{:S(2)}, u32[]{:S(2)}) collective-permute-start(bf16[32,64,256]{2,1,0:T(8,128)(2,1)} %all-gather.3.cloned.1.call-done), channel_id=1, source_target_pairs={{0,12},{4,0},{8,4},{12,8},{1,13},{5,1},{9,5},{13,9},{2,14},{6,2},{... | collective-permute-start | bytes 3145736 | tf_op jit(solution)/shard_map/ppermute | solution.py:55
  152.8 1.6 copy-start.3
  152.8 2.2 %copy-start.4 = (bf16[1,32,2,32,2,256]{5,1,2,0,3,4:T(8,128)(2,1)S(1)}, bf16[1,32,2,32,2,256]{5,1,2,0,3,4:T(8,128)(2,1)}, u32[]{:S(2)}) copy-start(bf16[1,32,2,32,2,256]{5,1,2,0,3,4:T(8,128)(2,1)} %maximum_bitcast_fusion) | copy-start | bytes 6291460
  163.3 21.2 %copy-start.1 = (s32[1,1,4,2]{2,3,1,0:T(2,128)S(1)}, s32[1,1,4,2]{2,3,1,0:T(2,128)}, u32[]{:S(2)}) copy-start(s32[1,1,4,2]{2,3,1,0:T(2,128)} %param.7) | copy-start | bytes 100
Sparse Core Ops, SparseCore 0:
  15.0 23.9 all-gather.2
  40.6 35.0 all-gather.4
